TPU v7x, 32 devices: a whole 2x2x4 slice. The times are simulated.
32 devices in a mesh: quad: 16 (over z, x, core), rows: 2 (over y).
Axes of the slice: x: 2, y: 2, z: 4, core: 2. Of those that a mesh axis runs over, the one named last changes fastest.
Arguments:
- solutions: bfloat16 [32, 2, 64, 16, 1280], P('quad', None, None, None, 'rows'), may hold values from -64 to 64
- angles: float32 [32], replicated, may hold values from -3.140625 to 3.140625
- qweights: float32 [2, 32], replicated, may hold values from -1 to 1
- neighbours: int32 [320, 8], P(('quad', 'rows')), may hold values from 0 to 319, as said below
- hblocks: bfloat16 [320, 64, 512], P(('quad', 'rows')), may hold values from -0.25 to 0.25
Outputs:
- h_moments: bfloat16 [1024, 20480], P(None, ('quad', 'rows'))
- ritz_matrices: float32 [512, 2, 2, 512], P('quad')
Inputs may be any that keep to these rules, and one draw needn't show every extreme that they name: neighbours[c, 0] = c, neighbours[c, 1] = min(c + 2, 319), neighbours[c, 2] = max(c - 2, 0); every entry lies within 2 of c.
All inputs are finite; a program needn't handle non-finite values.
Results may differ from a plain program's by a relative error of at most 0.0075.
Values may be sent and summed in bfloat16 or wider, within the bound.
A program may use at most 64 MiB of HBM per device.

v0:
```python
import jax
import jax.numpy as jnp
from jax import lax
from jax.sharding import PartitionSpec as P

LCOL = 64
QPTS = 32
KMOM = 8
NB = 8
HALO = 2


def extended(block, sides, width):
    for axis, dim in sides:
        count = lax.axis_size(axis)
        forward = [(i, i + 1) for i in range(count - 1)]
        backward = [(target, source) for source, target in forward]
        low = lax.ppermute(
            lax.slice_in_dim(block, block.shape[dim] - width, None, axis=dim), axis, forward
        )
        high = lax.ppermute(lax.slice_in_dim(block, 0, width, axis=dim), axis, backward)
        block = jnp.concatenate([low, block, high], axis=dim)
    return block


def moment_coefficients(angles, qweights):
    order = jnp.arange(KMOM, dtype=jnp.float32)[:, None]
    phase = order * angles[None, :]
    cosine = jnp.cos(phase)
    sine = jnp.sin(phase)
    real_coef = qweights[0][None, :] * cosine - qweights[1][None, :] * sine
    imag_coef = qweights[0][None, :] * sine + qweights[1][None, :] * cosine
    real_rows = jnp.stack([real_coef, -imag_coef], -1)
    imag_rows = jnp.stack([imag_coef, real_coef], -1)
    mixing = jnp.stack([real_rows, imag_rows], 0)
    return mixing.reshape(2 * KMOM, 2 * QPTS).astype(jnp.bfloat16)


def split_parts(product, half_cols, row_count):
    real_part = product[:row_count, :half_cols] + product[row_count:, half_cols:]
    imag_part = product[:row_count, half_cols:] - product[row_count:, :half_cols]
    return jnp.stack([real_part, imag_part], 1)


def gram_part(moments, applied, first_row, row_count, total_rows):
    half_cols = moments.shape[0] // 2
    chosen = jnp.concatenate(
        [
            lax.dynamic_slice_in_dim(moments, first_row, row_count, 0),
            lax.dynamic_slice_in_dim(moments, half_cols + first_row, row_count, 0),
        ],
        0,
    )
    contract = (((1,), (1,)), ((), ()))
    plain = lax.dot_general(chosen, moments, contract, preferred_element_type=jnp.float32)
    mixed = lax.dot_general(chosen, applied, contract, preferred_element_type=jnp.float32)
    ritz = jnp.stack(
        [split_parts(plain, half_cols, row_count), split_parts(mixed, half_cols, row_count)], 1
    )
    return ritz * (1.0 / total_rows)


def per_device(solutions, angles, qweights, neighbours, hblocks):
    groups = lax.axis_size("quad") * lax.axis_size("rows")
    rows_dev = solutions.shape[4]
    cells_dev = hblocks.shape[0]
    orbitals = hblocks.shape[1]
    half_cols = KMOM * LCOL
    mixing = moment_coefficients(angles, qweights)
    received = lax.all_to_all(solutions, "quad", split_axis=3, concat_axis=0, tiled=True)
    stacked = received.reshape(QPTS * 2, LCOL, received.shape[4])
    result = jnp.einsum("pq,qln->pln", mixing, stacked, preferred_element_type=jnp.float32)
    moments = result.reshape(2 * half_cols, received.shape[4]).astype(jnp.bfloat16)
    padded = extended(moments, ((("quad", "rows"), 1),), HALO * orbitals)
    first_cell = (
        lax.axis_index("quad") * lax.axis_size("rows") + lax.axis_index("rows")
    ) * cells_dev
    local_index = (neighbours - first_cell + HALO).reshape(-1)
    cellwise = padded.reshape(2 * half_cols, cells_dev + 2 * HALO, orbitals)
    nearby = jnp.take(cellwise, local_index, axis=1).reshape(
        2 * half_cols, cells_dev, NB * orbitals
    )
    applied = jnp.einsum("cam,xcm->xca", hblocks, nearby, preferred_element_type=jnp.float32)
    applied = applied.reshape(2 * half_cols, rows_dev).astype(jnp.bfloat16)
    total_rows = rows_dev * groups
    share_rows = half_cols // lax.axis_size("quad")
    summed = lax.psum(gram_part(moments, applied, 0, half_cols, total_rows), ("quad", "rows"))
    ritz_matrices = lax.dynamic_slice_in_dim(
        summed, lax.axis_index("quad") * share_rows, share_rows, 0
    )
    return (applied, ritz_matrices)


def solution(mesh):
    in_specs = (
        P("quad", None, None, None, "rows"),
        P(),
        P(),
        P(("quad", "rows"), None),
        P(("quad", "rows"), None, None),
    )
    out_specs = (P(None, ("quad", "rows")), P("quad", None, None, None))
    return jax.shard_map(
        per_device, mesh=mesh, in_specs=in_specs, out_specs=out_specs, check_vma=False
    )
```

profile of v0, /device:TPU:0, one launch (start us, length us, event | category | flops | bytes accessed | tf_op | source)
XLA Modules:
  0.0 333.4 jit_solution(11366127904357081607)
XLA Ops:
  7.2 6.2 %copy.34 = bf16[2,2,64,16,640]{4,2,1,0,3:T(8,128)(2,1)} copy(bf16[2,2,64,16,640]{4,3,2,1,0:T(8,128)(2,1)} %param.5) | data formatting | bytes 10485760 | tf_op args[0]
  13.3 7.5 %all-to-all-start = ((bf16[2,2,64,16,640]{4,2,1,0,3:T(8,128)(2,1)}), bf16[2,2,64,16,640]{4,2,1,0,3:T(8,128)(2,1)}, u32[]{:S(2)}, u32[]{:S(2)}) async-start(bf16[2,2,64,16,640]{4,2,1,0,3:T(8,128)(2,1)} %copy.34), calls=%async_computation | async-start | bytes 10485760 | tf_op jit(solution)/shard_map/all_to_all | solution.py:70
  21.8 95.1 %all-to-all-done = bf16[2,2,64,16,640]{4,2,1,0,3:T(8,128)(2,1)} async-done(((bf16[2,2,64,16,640]{4,2,1,0,3:T(8,128)(2,1)}), bf16[2,2,64,16,640]{4,2,1,0,3:T(8,128)(2,1)}, u32[]{:S(2)}, u32[]{:S(2)}) %all-to-all-start) | async-done | bytes 5242912 | tf_op jit(solution)/shard_map/all_to_all | solution.py:70
  116.8 6.5 %fusion.6 = bf16[16,64,640]{2,0,1:T(8,128)(2,1)S(1)} fusion(bf16[64,64,640]{2,1,0:T(8,128)(2,1)} %bitcast.7, bf16[16,64]{0,1:T(8,128)(2,1)S(1)} %convert_element_type.30), kind=kOutput, calls=%fused_computation.11 | convolution fusion | flops 84541440 | bytes 6555648 | tf_op jit(solution)/shard_map/pq,qln->pln/dot_general | solution.py:72
  123.3 0.3 copy.37
  123.7 1.8 fusion.23
  125.5 3.4 %collective-permute-start = (bf16[1024,128]{1,0:T(8,128)(2,1)S(1)}, bf16[1024,128]{1,0:T(8,128)(2,1)S(1)}, u32[]{:S(2)}, u32[]{:S(2)}) collective-permute-start(bf16[1024,128]{1,0:T(8,128)(2,1)S(1)} %get-tuple-element.14), channel_id=1, source_target_pairs={{0,1},{1,2},{2,3},{3,4},{4,5},{5,6},{6,7},{7,8},{8,9},{9,10},{10,1... | collective-permute-start | bytes 786440 | tf_op jit(solution)/shard_map/ppermute | solution.py:18
  128.9 1.5 collective-permute-start.1
  130.4 1.5 fusion.15
  131.9 3.7 %collective-permute-done = bf16[1024,128]{1,0:T(8,128)(2,1)S(1)} collective-permute-done((bf16[1024,128]{1,0:T(8,128)(2,1)S(1)}, bf16[1024,128]{1,0:T(8,128)(2,1)S(1)}, u32[]{:S(2)}, u32[]{:S(2)}) %collective-permute-start) | collective-permute-done | bytes 262176 | tf_op jit(solution)/shard_map/ppermute | solution.py:18
  135.6 1.6 collective-permute-done.1
  137.2 1.4 pad_maximum_fusion
  138.6 2.9 copy.38
  141.5 6.3 %gather_fusion = bf16[80,1024,64]{1,2,0:T(8,128)(2,1)} fusion(bf16[1024,14,64]{0,2,1:T(8,128)(2,1)S(1)} %bitcast.45, s32[1024]{0:T(1024)S(1)} %pad_clamp_fusion), kind=kCustom, calls=%fused_computation | custom fusion | bytes 20971840 | tf_op jit(solution)/shard_map/jit(_take)/gather | solution.py:80
  147.8 5.5 %fusion.9 = bf16[10,1024,64]{1,2,0:T(8,128)(2,1)S(1)} fusion(bf16[10,64,512]{2,1,0:T(8,128)(2,1)S(1)} %copy-done, bf16[1024,10,512]{0,2,1:T(8,128)(2,1)} %bitcast.46, pred[10,512]{1,0:T(8,128)(4,1)S(1)} %broadcast_in_dim.17), kind=kOutput, calls=%fused_computation.12 | convolution fusion | flops 676986880 | bytes 12456960 | tf_op jit(solution)/shard_map/cam,xcm->xca/dot_general | solution.py:83
  153.4 1.8 fusion.24
  155.2 0.5 fusion.13
  155.7 0.7 copy-done.3
  156.4 0.4 maximum_bitcast_fusion
  156.9 2.7 maximum_multiply_fusion
  159.6 1.4 copy.41
  161.1 163.6 %all-reduce.2.cloned.1.call-done = f32[512,2,2,512]{3,0,2,1:T(8,128)} async-done(((f32[512,2,2,512]{3,0,2,1:T(8,128)}), f32[512,2,2,512]{3,0,2,1:T(8,128)}) %all-reduce.2.cloned.1.call-update) | async-done | bytes 4194320 | tf_op jit(solution)/shard_map/psum | solution.py:87
  324.7 1.0 constant_dynamic-slice_fusion
  325.6 0.9 copy.42
  (31 shorter events, 0.9 us)
Async XLA Ops:
  7.2 140.7 %copy-start = (bf16[10,64,512]{2,1,0:T(8,128)(2,1)S(1)}, bf16[10,64,512]{2,1,0:T(8,128)(2,1)}, u32[]{:S(2)}) copy-start(bf16[10,64,512]{2,1,0:T(8,128)(2,1)} %param.9) | copy-start | bytes 1966084
  13.3 7.6 %copy-start.5 = (f32[2,32]{1,0:T(2,128)S(1)}, f32[2,32]{1,0:T(2,128)}, u32[]{:S(2)}) copy-start(f32[2,32]{1,0:T(2,128)} %param.7) | copy-start | bytes 772
  13.3 7.6 %copy-start.6 = (f32[32]{0:T(128)S(1)}, f32[32]{0:T(128)}, u32[]{:S(2)}) copy-start(f32[32]{0:T(128)} %param.6) | copy-start | bytes 388
  13.3 7.9 %copy-start.4 = (s32[10,8]{0,1:T(8,128)S(1)}, s32[10,8]{0,1:T(8,128)}, u32[]{:S(2)}) copy-start(s32[10,8]{0,1:T(8,128)} %param.8) | copy-start | bytes 964
  13.3 103.5 %all-to-all-start = ((bf16[2,2,64,16,640]{4,2,1,0,3:T(8,128)(2,1)}), bf16[2,2,64,16,640]{4,2,1,0,3:T(8,128)(2,1)}, u32[]{:S(2)}, u32[]{:S(2)}) async-start(bf16[2,2,64,16,640]{4,2,1,0,3:T(8,128)(2,1)} %copy.34), calls=%async_computation | async-start | bytes 10485760 | tf_op jit(solution)/shard_map/all_to_all | solution.py:70
  20.9 303.8 %all-reduce.2.cloned.1.call-start = ((), (), s32[]{:S(2)}) async-start(), calls=%async_computation.1 | async-start | bytes 8388608 | tf_op jit(solution)/shard_map/psum | solution.py:87
  123.6 13.6 %copy-start.1 = (bf16[16,64,640]{2,1,0:T(8,128)(2,1)}, bf16[16,64,640]{2,1,0:T(8,128)(2,1)S(1)}, u32[]{:S(2)}) copy-start(bf16[16,64,640]{2,1,0:T(8,128)(2,1)S(1)} %copy.37) | copy-start | bytes 3932164
  125.5 10.1 %collective-permute-start = (bf16[1024,128]{1,0:T(8,128)(2,1)S(1)}, bf16[1024,128]{1,0:T(8,128)(2,1)S(1)}, u32[]{:S(2)}, u32[]{:S(2)}) collective-permute-start(bf16[1024,128]{1,0:T(8,128)(2,1)S(1)} %get-tuple-element.14), channel_id=1, source_target_pairs={{0,1},{1,2},{2,3},{3,4},{4,5},{5,6},{6,7},{7,8},{8,9},{9,10},{10,1... | collective-permute-start | bytes 786440 | tf_op jit(solution)/shard_map/ppermute | solution.py:18
  128.9 8.3 %collective-permute-start.1 = (bf16[1024,128]{1,0:T(8,128)(2,1)S(1)}, bf16[1024,128]{1,0:T(8,128)(2,1)S(1)}, u32[]{:S(2)}, u32[]{:S(2)}) collective-permute-start(bf16[1024,128]{1,0:T(8,128)(2,1)S(1)} %get-tuple-element.15), channel_id=1, source_target_pairs={{1,0},{2,1},{3,2},{4,3},{5,4},{6,5},{7,6},{8,7},{9,8},{10,9},{11,1... | collective-permute-start | bytes 786440 | tf_op jit(solution)/shard_map/ppermute | solution.py:21
  147.8 5.6 %copy-start.2 = (bf16[16,64,640]{2,1,0:T(8,128)(2,1)S(1)}, bf16[16,64,640]{2,1,0:T(8,128)(2,1)}, u32[]{:S(2)}) copy-start(bf16[16,64,640]{2,1,0:T(8,128)(2,1)} %copy-done.1) | copy-start | bytes 3932164
  155.2 1.2 copy-start.3
Sparse Core Ops, SparseCore 0:
  159.7 164.8 all-reduce.1
where the time goes:
time: 334 us; the launch traced here: 333 us
  waiting for transfers between devices  264 us (79%)
  local copies, waits for them, and re-layouts  20.4 us (6%)
  matrix products  15.7 us (5%)
  between operations  14.2 us (4%)
  starting transfers between devices  12.5 us (4%)
  other arithmetic  6.65 us (2%)
    psum x1, waiting for transfers between devices, per_device(): lax.psum(gram_part(moments, applied, 0, half_cols, total_rows), ('quad',...  164 us
    all_to_all x1, waiting for transfers between devices, per_device(): lax.all_to_all(solutions, 'quad', split_axis=3, concat_axis=0, tiled=True)  95.1 us
    unnamed x17, local copies, waits for them, and re-layouts  9.26 us
    all_to_all x1, starting transfers between devices, per_device(): lax.all_to_all(solutions, 'quad', split_axis=3, concat_axis=0, tiled=True)  7.53 us
  transfers between devices with their start and end apart: 4, of which 4 were waited for; matrix products, arithmetic and copies ran while one was open for 1% of the time, Pallas kernels for 0%

commit v1 on v0

--- a/solution.py
+++ b/solution.py
@@ -67,7 +67,10 @@
     orbitals = hblocks.shape[1]
     half_cols = KMOM * LCOL
     mixing = moment_coefficients(angles, qweights)
-    received = lax.all_to_all(solutions, "quad", split_axis=3, concat_axis=0, tiled=True)
+    count_2 = lax.axis_size("quad")
+    blocks = jnp.stack(jnp.split(solutions, count_2, axis=3), axis=0)
+    blocks = lax.all_to_all(blocks, "quad", split_axis=0, concat_axis=0)
+    received = jnp.concatenate(blocks, axis=0)
     stacked = received.reshape(QPTS * 2, LCOL, received.shape[4])
     result = jnp.einsum("pq,qln->pln", mixing, stacked, preferred_element_type=jnp.float32)
     moments = result.reshape(2 * half_cols, received.shape[4]).astype(jnp.bfloat16)

time: 334 us -> 362 us (1.084)
  local copies, waits for them, and re-layouts: 20.4 us -> 48.1 us
    split x0 -> x1, local copies, waits for them, and re-layouts: none -> 21.4 us  [per_device(): blocks = jnp.stack(jnp.split(solutions, count_2, axis=3), axis=0)]
    unnamed x17 -> x31, local copies, waits for them, and re-layouts: 9.26 us -> 14.8 us
where the time goes in v1:
time: 362 us; the launch traced here: 361 us
  waiting for transfers between devices  264 us (73%)
  local copies, waits for them, and re-layouts  48.1 us (13%)
  matrix products  15.7 us (4%)
  between operations  14.3 us (4%)
  starting transfers between devices  12.5 us (3%)
  other arithmetic  6.63 us (2%)
    psum x1, waiting for transfers between devices, per_device(): lax.psum(gram_part(moments, applied, 0, half_cols, total_rows), ('quad',...  164 us
    all_to_all x1, waiting for transfers between devices, per_device(): blocks = lax.all_to_all(blocks, 'quad', split_axis=0, concat_axis=0)  95.1 us
    split x1, local copies, waits for them, and re-layouts, per_device(): blocks = jnp.stack(jnp.split(solutions, count_2, axis=3), axis=0)  21.4 us
    unnamed x31, local copies, waits for them, and re-layouts  14.8 us
    all_to_all x1, starting transfers between devices, per_device(): blocks = lax.all_to_all(blocks, 'quad', split_axis=0, concat_axis=0)  7.53 us
  transfers between devices with their start and end apart: 4, of which 4 were waited for; matrix products, arithmetic and copies ran while one was open for 1% of the time, Pallas kernels for 0%

profile of v1, /device:TPU:0, one launch (start us, length us, event | category | flops | bytes accessed | tf_op | source)
XLA Modules:
  0.0 361.1 jit_solution(4098353681570204009)
XLA Ops:
  7.2 21.4 %fusion.38 = (bf16[2,2,64,1,640]{4,3,2,1,0:T(2,128)(2,1)S(1)}, bf16[2,2,64,1,640]{4,3,2,1,0:T(2,128)(2,1)S(1)}, bf16[2,2,64,1,640]{4,3,2,1,0:T(2,128)(2,1)S(1)},...) fusion(bf16[2,2,64,16,640]{4,3,2,1,0:T(8,128)(2,1)} %param.5), kind=kLoop, calls=%fused_computation.74 | loop fusion | bytes 10485760 | tf_op jit(solution)/shard_map/split | solution.py:71
  34.8 0.8 fusion.23
  35.6 0.8 fusion.22
  36.4 0.8 fusion.21
  37.2 0.8 fusion.20
  41.1 7.5 %all-to-all-start = ((bf16[16,2,2,64,1,640]{5,3,2,1,4,0:T(8,128)(2,1)}), bf16[16,2,2,64,1,640]{5,3,2,1,4,0:T(8,128)(2,1)}, u32[]{:S(2)}, u32[]{:S(2)}) async-start(bf16[16,2,2,64,1,640]{5,3,2,1,4,0:T(8,128)(2,1)} %fusion.16), calls=%async_computation | async-start | bytes 10485760 | tf_op jit(solution)/shard_map/all_to_all | solution.py:72
  49.5 95.1 %all-to-all-done = bf16[16,2,2,64,1,640]{5,3,2,1,4,0:T(8,128)(2,1)} async-done(((bf16[16,2,2,64,1,640]{5,3,2,1,4,0:T(8,128)(2,1)}), bf16[16,2,2,64,1,640]{5,3,2,1,4,0:T(8,128)(2,1)}, u32[]{:S(2)}, u32[]{:S(2)}) %all-to-all-start) | async-done | bytes 5242912 | tf_op jit(solution)/shard_map/all_to_all | solution.py:72
  144.6 6.5 %fusion.6 = bf16[16,64,640]{2,0,1:T(8,128)(2,1)S(1)} fusion(bf16[64,64,640]{2,1,0:T(8,128)(2,1)} %bitcast.21, bf16[16,64]{0,1:T(8,128)(2,1)S(1)} %convert_element_type.30), kind=kOutput, calls=%fused_computation.11 | convolution fusion | flops 84541440 | bytes 6555648 | tf_op jit(solution)/shard_map/pq,qln->pln/dot_general | solution.py:75
  151.4 1.8 fusion.40
  153.2 3.4 collective-permute-start
  156.7 1.5 collective-permute-start.1
  158.2 1.5 fusion.15
  159.6 3.7 %collective-permute-done = bf16[1024,128]{1,0:T(8,128)(2,1)S(1)} collective-permute-done((bf16[1024,128]{1,0:T(8,128)(2,1)S(1)}, bf16[1024,128]{1,0:T(8,128)(2,1)S(1)}, u32[]{:S(2)}, u32[]{:S(2)}) %collective-permute-start) | collective-permute-done | bytes 262176 | tf_op jit(solution)/shard_map/ppermute | solution.py:18
  163.4 1.6 collective-permute-done.1
  165.0 1.4 pad_maximum_fusion
  166.4 2.9 copy.74
  169.3 6.3 %gather_fusion = bf16[80,1024,64]{1,2,0:T(8,128)(2,1)} fusion(bf16[1024,14,64]{0,2,1:T(8,128)(2,1)S(1)} %bitcast.105, s32[1024]{0:T(1024)S(1)} %pad_clamp_fusion), kind=kCustom, calls=%fused_computation | custom fusion | bytes 20971840 | tf_op jit(solution)/shard_map/jit(_take)/gather | solution.py:83
  175.6 5.5 %fusion.9 = bf16[10,1024,64]{1,2,0:T(8,128)(2,1)S(1)} fusion(bf16[10,64,512]{2,1,0:T(8,128)(2,1)S(1)} %copy-done, bf16[1024,10,512]{0,2,1:T(8,128)(2,1)} %bitcast.106, pred[10,512]{1,0:T(8,128)(4,1)S(1)} %broadcast_in_dim.17), kind=kOutput, calls=%fused_computation.12 | convolution fusion | flops 676986880 | bytes 12456960 | tf_op jit(solution)/shard_map/cam,xcm->xca/dot_general | solution.py:86
  181.1 1.8 fusion.41
  184.6 2.7 maximum_multiply_fusion
  187.4 1.4 copy.77
  188.8 163.6 %all-reduce.2.cloned.1.call-done = f32[512,2,2,512]{3,0,2,1:T(8,128)} async-done(((f32[512,2,2,512]{3,0,2,1:T(8,128)}), f32[512,2,2,512]{3,0,2,1:T(8,128)}) %all-reduce.2.cloned.1.call-update) | async-done | bytes 4194320 | tf_op jit(solution)/shard_map/psum | solution.py:90
  352.4 1.0 constant_dynamic-slice_fusion
  353.4 0.9 copy.78
  (47 shorter events, 12.0 us)
Async XLA Ops:
  7.2 168.4 %copy-start = (bf16[10,64,512]{2,1,0:T(8,128)(2,1)S(1)}, bf16[10,64,512]{2,1,0:T(8,128)(2,1)}, u32[]{:S(2)}) copy-start(bf16[10,64,512]{2,1,0:T(8,128)(2,1)} %param.9) | copy-start | bytes 1966084
  41.1 7.6 %copy-start.5 = (f32[2,32]{1,0:T(2,128)S(1)}, f32[2,32]{1,0:T(2,128)}, u32[]{:S(2)}) copy-start(f32[2,32]{1,0:T(2,128)} %param.7) | copy-start | bytes 772
  41.1 7.6 %copy-start.6 = (f32[32]{0:T(128)S(1)}, f32[32]{0:T(128)}, u32[]{:S(2)}) copy-start(f32[32]{0:T(128)} %param.6) | copy-start | bytes 388
  41.1 7.9 %copy-start.4 = (s32[10,8]{0,1:T(8,128)S(1)}, s32[10,8]{0,1:T(8,128)}, u32[]{:S(2)}) copy-start(s32[10,8]{0,1:T(8,128)} %param.8) | copy-start | bytes 964
  41.1 103.5 %all-to-all-start = ((bf16[16,2,2,64,1,640]{5,3,2,1,4,0:T(8,128)(2,1)}), bf16[16,2,2,64,1,640]{5,3,2,1,4,0:T(8,128)(2,1)}, u32[]{:S(2)}, u32[]{:S(2)}) async-start(bf16[16,2,2,64,1,640]{5,3,2,1,4,0:T(8,128)(2,1)} %fusion.16), calls=%async_computation | async-start | bytes 10485760 | tf_op jit(solution)/shard_map/all_to_all | solution.py:72
  48.6 303.8 %all-reduce.2.cloned.1.call-start = ((), (), s32[]{:S(2)}) async-start(), calls=%async_computation.1 | async-start | bytes 8388608 | tf_op jit(solution)/shard_map/psum | solution.py:90
  151.4 13.6 %copy-start.1 = (bf16[16,64,640]{2,1,0:T(8,128)(2,1)}, bf16[16,64,640]{2,1,0:T(8,128)(2,1)S(1)}, u32[]{:S(2)}) copy-start(bf16[16,64,640]{2,1,0:T(8,128)(2,1)S(1)} %copy.73) | copy-start | bytes 3932164
  153.2 10.1 %collective-permute-start = (bf16[1024,128]{1,0:T(8,128)(2,1)S(1)}, bf16[1024,128]{1,0:T(8,128)(2,1)S(1)}, u32[]{:S(2)}, u32[]{:S(2)}) collective-permute-start(bf16[1024,128]{1,0:T(8,128)(2,1)S(1)} %get-tuple-element.28), channel_id=1, source_target_pairs={{0,1},{1,2},{2,3},{3,4},{4,5},{5,6},{6,7},{7,8},{8,9},{9,10},{10,1... | collective-permute-start | bytes 786440 | tf_op jit(solution)/shard_map/ppermute | solution.py:18
  156.7 8.3 %collective-permute-start.1 = (bf16[1024,128]{1,0:T(8,128)(2,1)S(1)}, bf16[1024,128]{1,0:T(8,128)(2,1)S(1)}, u32[]{:S(2)}, u32[]{:S(2)}) collective-permute-start(bf16[1024,128]{1,0:T(8,128)(2,1)S(1)} %get-tuple-element.29), channel_id=1, source_target_pairs={{1,0},{2,1},{3,2},{4,3},{5,4},{6,5},{7,6},{8,7},{9,8},{10,9},{11,1... | collective-permute-start | bytes 786440 | tf_op jit(solution)/shard_map/ppermute | solution.py:21
  175.6 5.5 %copy-start.2 = (bf16[16,64,640]{2,1,0:T(8,128)(2,1)S(1)}, bf16[16,64,640]{2,1,0:T(8,128)(2,1)}, u32[]{:S(2)}) copy-start(bf16[16,64,640]{2,1,0:T(8,128)(2,1)} %copy-done.1) | copy-start | bytes 3932164
  182.9 1.2 copy-start.3
Sparse Core Ops, SparseCore 0:
  187.5 164.8 all-reduce.1
